TPU v7x, 32 devices: a whole 2x2x4 slice. The times are simulated.
32 devices in a mesh: groups: 2 (over x), seq: 16 (over z, y, core).
Axes of the slice: x: 2, y: 2, z: 4, core: 2. Of those that a mesh axis runs over, the one named last changes fastest.
Arguments:
- queries: bfloat16 [8192, 1024], P(('groups', 'seq')), parts along dimension 0, may hold values from -6 to 6
- keys: bfloat16 [8192, 1024], P(('groups', 'seq')), parts along dimension 0, may hold values from -6 to 6
- values: bfloat16 [8192, 1024], P(('groups', 'seq')), parts along dimension 0, may hold values from -6 to 6
- out_grad: bfloat16 [8192, 1024], P(('groups', 'seq')), parts along dimension 0, may hold values from -0.09375 to 0.09375
- maps: float32 [2, 8, 128, 128], replicated, may hold values from -0.5 to 0.5
- gain: bfloat16 [1024], replicated, may hold values from 0.25 to 1.75
- first_moment: float32 [2048, 128], P('seq'), may hold values from -1.8 to 1.8
- second_moment: float32 [2048, 128], P('seq'), may hold values from 0.01 to 0.3
Outputs:
- attention: bfloat16 [8192, 1024], P(('groups', 'seq')), parts along dimension 0
- new_maps: float32 [4, 8, 128, 128], P('groups'), parts along dimension 0
- new_moments: float32 [4, 2048, 128], P('groups', 'seq'), parts along dimension 0
There are 2 independent parts, one for each index of `groups`. A program takes and returns all parts, laid end to end along the dimension named above; an argument that names none is the same for every part. Nothing has to cross between parts.
All inputs are finite; a program needn't handle non-finite values.
Results may differ from a plain program's by a relative error of at most 0.0057.
Values sent between devices are 32-bit elements; how exact they have to be, the bound alone decides.
A program may use at most 320 MiB of HBM per device.

v0:
```python
import jax
import jax.numpy as jnp
from jax import lax
from jax.sharding import PartitionSpec as P

H = 8
E = 128
SPAN = 256
OPT_STEP = 10


BETA_ONE = 0.9
BETA_TWO = 0.95
RATE = 0.01
TINY = 1e-08
NORM_EPS = 1e-06


def prefix(value, axis, join, neutral, backward):
    count, mine = (lax.axis_size(axis), lax.axis_index(axis))
    pieces = lax.all_gather(value, axis)
    if backward:
        pieces = pieces[::-1]
        mine = count - 1 - mine
    total = jnp.full_like(value, 0) + jnp.asarray(neutral, value.dtype)

    def lap(position, total):
        longer = join(total, pieces[position])
        return jnp.where(position < mine, longer, total)

    return lax.fori_loop(0, count - 1, lap, total)


def add_states(earlier, latter):
    return earlier + latter


def silu_slope(preact):
    sigmoid = jax.nn.sigmoid(preact)
    return sigmoid * (1.0 + preact * (1.0 - sigmoid))


def adam_rows(gradient, weights, first_old, second_old):
    first_new = BETA_ONE * first_old + (1.0 - BETA_ONE) * gradient
    second_new = BETA_TWO * second_old + (1.0 - BETA_TWO) * gradient * gradient
    first_hat = first_new / (1.0 - BETA_ONE**OPT_STEP)
    second_hat = second_new / (1.0 - BETA_TWO**OPT_STEP)
    return (weights - RATE * first_hat / (jnp.sqrt(second_hat) + TINY), first_new, second_new)


def product(form, left, right):
    return jnp.einsum(form, left, right, preferred_element_type=jnp.float32)


def local(queries, keys, values, out_grad, maps, gain, first_moment, second_moment):
    tok_rows = queries.shape[0]
    blocks = tok_rows // SPAN

    def arrange(tensor):
        return tensor.reshape(blocks, SPAN, H, E)

    query_in = arrange(queries)
    key_in = arrange(keys)
    value_in = arrange(values)
    grad_in = arrange(out_grad)
    low_maps = maps.astype(jnp.bfloat16)
    pre_query = product("nche,hef->nchf", query_in, low_maps[0])
    pre_key = product("nche,hef->nchf", key_in, low_maps[1])
    feat_query = jax.nn.silu(pre_query).astype(jnp.bfloat16)
    feat_key = jax.nn.silu(pre_key).astype(jnp.bfloat16)
    own_states = product("ncht,ncho->nhto", feat_key, value_in)
    zero_state = jnp.zeros((H, E, E), jnp.float32)
    start_state = prefix(jnp.sum(own_states, 0), "seq", add_states, zero_state, False)
    places = jnp.arange(SPAN)
    masked = (places[:, None] >= places[None, :])[None, None]
    scores = jnp.where(masked, product("ncht,nsht->nhcs", feat_query, feat_key), 0.0).astype(
        jnp.bfloat16
    )
    intra = product("nhcs,nsho->ncho", scores, value_in)
    before = (start_state[None] + jnp.cumsum(own_states, 0) - own_states).astype(jnp.bfloat16)
    raw = product("ncht,nhto->ncho", feat_query, before) + intra
    scale = lax.rsqrt(jnp.mean(raw * raw, -1, keepdims=True) + NORM_EPS)
    unit = raw * scale
    gain_wide = gain.reshape(H, E).astype(jnp.float32)
    attention = (unit * gain_wide).astype(jnp.bfloat16).reshape(tok_rows, H * E)
    dunit = grad_in.astype(jnp.float32) * gain_wide
    grad_raw = (scale * (dunit - unit * jnp.mean(dunit * unit, -1, keepdims=True))).astype(
        jnp.bfloat16
    )
    grad_states = product("ncht,ncho->nhto", feat_query, grad_raw)
    after_state = prefix(jnp.sum(grad_states, 0), "seq", add_states, zero_state, True)
    pscores = jnp.where(masked, product("ncho,nsho->nhcs", grad_raw, value_in), 0.0).astype(
        jnp.bfloat16
    )
    grad_fq = product("ncho,nhto->ncht", grad_raw, before) + product(
        "nhcs,nsht->ncht", pscores, feat_key
    )
    local_fk = product("nhcs,ncht->nsht", pscores, feat_query)
    after = (after_state[None] + jnp.sum(grad_states, 0)[None] - jnp.cumsum(grad_states, 0)).astype(
        jnp.bfloat16
    )
    grad_fk = product("ncho,nhto->ncht", value_in, after) + local_fk
    grad_pq = (grad_fq * silu_slope(pre_query)).astype(jnp.bfloat16)
    grad_pk = (grad_fk * silu_slope(pre_key)).astype(jnp.bfloat16)
    grad_query = product("ncht,nchu->htu", query_in, grad_pq)
    grad_key = product("ncht,nchu->htu", key_in, grad_pk)
    local_grad = jnp.stack([grad_query, grad_key]).reshape(2 * H * E, E)
    share = 2 * H * E // lax.axis_size("seq")
    offset = lax.axis_index("seq") * share
    flat_maps = maps.reshape(2 * H * E, E)
    own_grad = lax.psum_scatter(local_grad, "seq", scatter_dimension=0, tiled=True)
    own_maps = lax.dynamic_slice_in_dim(flat_maps, offset, share, 0)
    new_part, first_new, second_new = adam_rows(own_grad, own_maps, first_moment, second_moment)
    new_flat = lax.all_gather(new_part, "seq", axis=0, tiled=True)
    new_maps = new_flat.reshape(2, H, E, E)
    return (attention, new_maps, jnp.stack([first_new, second_new]))


def solution(mesh):
    in_specs = (
        P(("groups", "seq"), None),
        P(("groups", "seq"), None),
        P(("groups", "seq"), None),
        P(("groups", "seq"), None),
        P(),
        P(),
        P("seq", None),
        P("seq", None),
    )
    out_specs = (
        P(("groups", "seq"), None),
        P("groups", None, None, None),
        P("groups", "seq", None),
    )
    return jax.shard_map(local, mesh=mesh, in_specs=in_specs, out_specs=out_specs, check_vma=False)
```

profile of v0, /device:TPU:0, one launch (start us, length us, event | category | flops | bytes accessed | tf_op | source)
XLA Modules:
  0.0 324.3 jit_solution(4487433849518444684)
XLA Ops:
  7.2 0.0 all-gather.8.cloned.1.call-start
  7.2 1.3 copy.54
  8.5 1.7 copy.29
  10.2 0.3 convolution_bitcast_fusion.1
  10.5 1.2 fusion.21
  11.8 0.0 all-gather.10.cloned.1.call-start
  11.9 2.0 copy.55
  13.9 0.2 copy.36
  14.2 2.4 multiply_convert_fusion.2
  16.5 73.0 %all-gather.8.cloned.1.call-done = f32[128,128,128]{2,1,0:T(8,128)} async-done(((f32[8,128,128]{2,1,0:T(8,128)}), f32[128,128,128]{2,1,0:T(8,128)}) %all-gather.8.cloned.1.call-update) | async-done | bytes 8388624 | tf_op jit(solution)/shard_map/all_gather | solution.py:21
  89.5 18.8 %while.28 = (s32[]{:T(128)}, f32[8,128,128]{2,1,0:T(8,128)S(1)}, s32[]{:T(128)}, f32[16,8,128,128]{3,2,1,0:T(8,128)}, s32[]{:T(128)}, /*index=5*/s32[]{:T(128)}) while((s32[]{:T(128)}, f32[8,128,128]{2,1,0:T(8,128)S(1)}, s32[]{:T(128)}, f32[16,8,128,128]{3,2,1,0:T(8,128)}, s32[]{:T(128)}, /*index=5*/s32[]{:T(128)}) %tuple.86), condition=%wide.region_1.2_spmd.clone, body=%wide.region_0.1_spmd.clone.sunk | while | flops 393220 | bytes 1572957 | solution.py:31
  89.5 1.3 add_select_fusion.4
  90.9 1.2 add_select_fusion.4
  92.1 1.2 add_select_fusion.4
  93.4 1.2 add_select_fusion.4
  94.6 1.2 add_select_fusion.4
  95.9 1.2 add_select_fusion.4
  97.1 1.2 add_select_fusion.4
  98.4 1.2 add_select_fusion.4
  99.6 1.2 add_select_fusion.4
  100.9 1.2 add_select_fusion.4
  102.1 1.2 add_select_fusion.4
  103.4 1.2 add_select_fusion.4
  104.6 1.2 add_select_fusion.4
  105.9 1.2 add_select_fusion.4
  107.1 1.2 add_select_fusion.4
  108.4 0.1 fusion.14
  108.4 1.4 fusion.29
  109.8 2.5 multiply_reduce_fusion.1
  112.4 0.3 multiply_reduce_fusion
  112.7 1.1 fusion.16
  113.8 1.1 fusion.25
  114.9 0.0 reduce-scatter.2.cloned.1.call-start
  115.0 1.4 fusion.53
  116.4 1.5 select_convert_fusion
  117.8 3.6 %convolution_bitcast_fusion.3 = f32[1,8,128,128]{3,2,1,0:T(8,128)} fusion(bf16[256,8,128]{0,2,1:T(8,128)(2,1)S(1)} %bitcast.162, f32[8,128,256]{2,1,0:T(8,128)} %fusion.53, bf16[8,256,256]{2,1,0:T(8,128)(2,1)} %select_convert_fusion, f32[1,256,8,128]{1,3,2,0:T(8,128)} %get-tuple-element.221, f32[1,256,8,128]{1,3,2,0:T(8,128)S(1)} %copy-done.10), kind=kOutput, calls=%fused_computation.21 | convolution fusion | flops 205258752 | bytes 5242880 | tf_op jit(solution)/shard_map/ncht,nchu->htu/dot_general | solution.py:52
  121.4 66.8 %all-gather.10.cloned.1.call-done = f32[128,128,128]{2,1,0:T(8,128)} async-done(((f32[8,128,128]{2,1,0:T(8,128)}), f32[128,128,128]{2,1,0:T(8,128)}) %all-gather.10.cloned.1.call-update) | async-done | bytes 8388624 | tf_op jit(solution)/shard_map/all_gather | solution.py:21
  188.2 7.7 %rev.3 = f32[16,8,128,128]{3,2,1,0:T(8,128)} reverse(f32[16,8,128,128]{3,2,1,0:T(8,128)} %bitcast.153), dimensions={0} | reverse | bytes 16777216 | tf_op jit(solution)/shard_map/rev | solution.py:23
  195.9 18.8 %while.29 = (s32[]{:T(128)}, f32[8,128,128]{2,1,0:T(8,128)S(1)}, s32[]{:T(128)}, f32[16,8,128,128]{3,2,1,0:T(8,128)}, s32[]{:T(128)}, /*index=5*/s32[]{:T(128)}) while((s32[]{:T(128)}, f32[8,128,128]{2,1,0:T(8,128)S(1)}, s32[]{:T(128)}, f32[16,8,128,128]{3,2,1,0:T(8,128)}, s32[]{:T(128)}, /*index=5*/s32[]{:T(128)}) %tuple.73), condition=%wide.region_5.6_spmd.clone, body=%wide.region_4.5_spmd.clone.sunk | while | flops 393220 | bytes 1572957 | solution.py:31
  195.9 1.3 add_select_fusion.5
  197.2 1.2 add_select_fusion.5
  198.5 1.2 add_select_fusion.5
  199.7 1.2 add_select_fusion.5
  201.0 1.2 add_select_fusion.5
  202.2 1.2 add_select_fusion.5
  203.5 1.2 add_select_fusion.5
  204.7 1.2 add_select_fusion.5
  206.0 1.2 add_select_fusion.5
  207.2 1.2 add_select_fusion.5
  208.5 1.2 add_select_fusion.5
  209.8 1.2 add_select_fusion.5
  211.0 1.2 add_select_fusion.5
  212.3 1.2 add_select_fusion.5
  213.5 1.2 add_select_fusion.5
  214.8 1.3 fusion.18
  216.1 2.7 convolution_bitcast_fusion.2
  218.8 1.0 pad_maximum_fusion
  219.9 0.0 all-gather.6.cloned.1.call-start
  219.9 55.7 %reduce-scatter.2.cloned.1.call-done = f32[128,128]{1,0:T(8,128)} async-done(((f32[2048,128]{1,0:T(8,128)}), f32[128,128]{1,0:T(8,128)}) %reduce-scatter.2.cloned.1.call-update) | async-done | bytes 65552 | tf_op jit(solution)/shard_map/reduce_scatter | solution.py:111
  275.7 1.6 fusion.44
  277.3 1.0 copy.46
  278.3 0.7 pad_maximum_fusion.1
  279.0 36.6 %all-gather.6.cloned.1.call-done = f32[2048,128]{1,0:T(8,128)} async-done(((f32[128,128]{1,0:T(8,128)}), f32[2048,128]{1,0:T(8,128)}) %all-gather.6.cloned.1.call-update) | async-done | bytes 1048592 | tf_op jit(solution)/shard_map/all_gather | solution.py:114
  315.5 2.3 copy.88
  (44 shorter events, 0.2 us)
Async XLA Ops:
  7.2 3.4 %copy-start = (bf16[256,1024]{1,0:T(8,128)(2,1)S(1)}, bf16[256,1024]{1,0:T(8,128)(2,1)}, u32[]{:S(2)}) copy-start(bf16[256,1024]{1,0:T(8,128)(2,1)} %param.14) | copy-start | bytes 1572868
  7.2 82.4 %all-gather.8.cloned.1.call-start = ((), (), s32[]{:S(2)}) async-start(), calls=%async_computation.3 | async-start | bytes 8912896 | tf_op jit(solution)/shard_map/all_gather | solution.py:21
  8.5 3.2 copy-start.5
  10.5 1.3 copy-start.9
  10.5 3.4 %copy-start.11 = (bf16[256,1024]{1,0:T(8,128)(2,1)S(1)}, bf16[256,1024]{1,0:T(8,128)(2,1)}, u32[]{:S(2)}) copy-start(bf16[256,1024]{1,0:T(8,128)(2,1)} %param.15) | copy-start | bytes 1572868
  11.8 2.4 copy-start.16
  11.8 176.4 %all-gather.10.cloned.1.call-start = ((), (), s32[]{:S(2)}) async-start(), calls=%async_computation.4 | async-start | bytes 8912896 | tf_op jit(solution)/shard_map/all_gather | solution.py:21
  16.5 91.9 %copy-start.2 = (bf16[1,256,8,128]{1,3,2,0:T(8,128)(2,1)}, bf16[1,256,8,128]{1,3,2,0:T(8,128)(2,1)S(1)}, u32[]{:S(2)}) copy-start(bf16[1,256,8,128]{1,3,2,0:T(8,128)(2,1)S(1)} %get-tuple-element.220) | copy-start | bytes 1572868
  89.5 18.8 %copy-start.7 = (f32[8,128,128]{2,1,0:T(8,128)S(1)}, f32[8,128,128]{2,1,0:T(8,128)}, u32[]{:S(2)}) copy-start(f32[8,128,128]{2,1,0:T(8,128)} %fusion.21) | copy-start | bytes 1572868
  112.6 1.1 copy-start.3
  114.9 2.9 copy-start.10
  114.9 2.9 copy-start.12
  114.9 160.7 %reduce-scatter.2.cloned.1.call-start = ((), (), s32[]{:S(2)}) async-start(), calls=%async_computation.1 | async-start | bytes 1114112 | tf_op jit(solution)/shard_map/reduce_scatter | solution.py:111
  195.9 18.8 %copy-start.1 = (f32[8,128,128]{2,1,0:T(8,128)S(1)}, f32[8,128,128]{2,1,0:T(8,128)}, u32[]{:S(2)}) copy-start(f32[8,128,128]{2,1,0:T(8,128)} %fusion.25) | copy-start | bytes 1572868
  214.7 1.3 copy-start.4
  214.8 1.3 copy-start.6
  216.1 2.7 copy-start.13
  218.8 56.9 %copy-start.14 = (f32[128,128]{1,0:T(8,128)S(1)}, f32[128,128]{1,0:T(8,128)}, u32[]{:S(2)}) copy-start(f32[128,128]{1,0:T(8,128)} %param.18) | copy-start | bytes 196612
  218.8 56.9 %copy-start.15 = (f32[128,128]{1,0:T(8,128)S(1)}, f32[128,128]{1,0:T(8,128)}, u32[]{:S(2)}) copy-start(f32[128,128]{1,0:T(8,128)} %param.19) | copy-start | bytes 196612
  218.8 58.5 %copy-start.8 = (bf16[1,256,8,128]{1,3,2,0:T(8,128)(2,1)S(1)}, bf16[1,256,8,128]{1,3,2,0:T(8,128)(2,1)}, u32[]{:S(2)}) copy-start(bf16[1,256,8,128]{1,3,2,0:T(8,128)(2,1)} %get-tuple-element.216) | copy-start | bytes 1572868
  219.9 95.6 %all-gather.6.cloned.1.call-start = ((), (), s32[]{:S(2)}) async-start(), calls=%async_computation.2 | async-start | bytes 1114112 | tf_op jit(solution)/shard_map/all_gather | solution.py:114
Sparse Core Ops, SparseCore 0:
  11.9 77.5 all-gather.7
  115.0 73.1 all-gather.9
  220.0 55.6 reduce-scatter.1
  278.5 36.9 all-gather.5
where the time goes:
time: 326 us; the launch traced here: 324 us
  waiting for transfers between devices  232 us (71%)
  other arithmetic  41.7 us (13%)
  matrix products  19.2 us (6%)
  local copies, waits for them, and re-layouts  16.3 us (5%)
  between operations  14 us (4%)
    all_gather x2, waiting for transfers between devices, prefix(): pieces = lax.all_gather(value, axis)  140 us
    reduce_scatter x1, waiting for transfers between devices, local(): lax.psum_scatter(local_grad, 'seq', scatter_dimension=0, tiled=True)  55.7 us
    select_n x30, other arithmetic, lap(): return jnp.where(position < mine, longer, total)  36.9 us
    all_gather x1, waiting for transfers between devices, local(): new_flat = lax.all_gather(new_part, 'seq', axis=0, tiled=True)  36.6 us
    dot_general x11, matrix products, product(): return jnp.einsum(form, left, right, preferred_element_type=jnp.float32)  19.2 us
    rev x1, local copies, waits for them, and re-layouts, prefix(): pieces = pieces[::-1]  7.71 us
  transfers between devices with their start and end apart: 4, of which 4 were waited for; matrix products, arithmetic and copies ran while one was open for 4% of the time, Pallas kernels for 0%

commit v1 on v0

v1 whole, which is shorter than its diff:
```python
import functools

import jax
import jax.numpy as jnp
from jax import lax
from jax.experimental import pallas as pl
from jax.experimental.pallas import tpu as pltpu
from jax.sharding import PartitionSpec as P

H = 8
E = 128
SPAN = 256
OPT_STEP = 10
CHUNKS = 2

BETA_ONE = 0.9
BETA_TWO = 0.95
RATE = 0.01
TINY = 1e-08
NORM_EPS = 1e-06

F32 = jnp.float32
BF16 = jnp.bfloat16


def dot(left, right, left_dim, right_dim):
    return lax.dot_general(
        left, right, (((left_dim,), (right_dim,)), ((), ())), preferred_element_type=F32
    )


def adam_rows(gradient, weights, first_old, second_old):
    first_new = BETA_ONE * first_old + (1.0 - BETA_ONE) * gradient
    second_new = BETA_TWO * second_old + (1.0 - BETA_TWO) * gradient * gradient
    first_hat = first_new / (1.0 - BETA_ONE**OPT_STEP)
    second_hat = second_new / (1.0 - BETA_TWO**OPT_STEP)
    return (weights - RATE * first_hat / (jnp.sqrt(second_hat) + TINY), first_new, second_new)


def layout(count):
    chips = count // 2
    row = 1
    while row * row * 4 <= chips:
        row *= 2
    plane = 2 * row
    return count // plane, plane


def kernel(
    depth, plane, share,
    queries, keys, values, out_grad, maps, gain, first_old, second_old,
    attention, new_maps, new_moments,
    feat_q, feat_k, slope_q, slope_k, raw_part, grad_raw, local_fk,
    states, plane_in, chain_in, chain_out, back, summed,
    grads, grads_in, grads_part, rows_in,
    send_a, recv_a, send_z, recv_z, send_c, recv_c,
    send_r, recv_r, send_rz, recv_rz, send_g, recv_g, send_p, recv_p,
):
    group = lax.axis_index("groups")
    me = lax.axis_index("seq")
    level = me // plane
    place = me % plane
    half = depth // 2
    rows = H * E // plane
    part = rows // CHUNKS
    peers = [(place + step) % plane for step in range(1, plane)]
    levels = [(level + step) % depth for step in range(1, depth)]

    def remote(src, dst, send, recv, to_level, to_place):
        return pltpu.make_async_remote_copy(
            src_ref=src, dst_ref=dst, send_sem=send, recv_sem=recv,
            device_id=(group, to_level * plane + to_place),
            device_id_type=pl.DeviceIdType.MESH,
        )

    def span(start, size):
        return pl.ds(pl.multiple_of(start, size), size)

    barrier = pltpu.get_barrier_semaphore()
    for peer in peers:
        pl.semaphore_signal(
            barrier, inc=1, device_id=(group, level * plane + peer),
            device_id_type=pl.DeviceIdType.MESH,
        )
    for other in levels:
        pl.semaphore_signal(
            barrier, inc=1, device_id=(group, other * plane + place),
            device_id_type=pl.DeviceIdType.MESH,
        )

    def heads(body):
        def pair(step, carry):
            body(2 * step)
            body(2 * step + 1)
            return carry

        lax.fori_loop(0, H // 2, pair, 0)

    def masked(scores):
        row = lax.broadcasted_iota(jnp.int32, (SPAN, SPAN), 0)
        column = lax.broadcasted_iota(jnp.int32, (SPAN, SPAN), 1)
        return jnp.where(row >= column, scores, 0.0).astype(BF16)

    def features(head):
        cols = span(head * E, E)

        def one(source, weights, feat, slope):
            pre = dot(source[:, cols], weights.astype(BF16), 1, 0)
            sigmoid = 1.0 / (1.0 + jnp.exp(-pre))
            feat[:, cols] = (pre * sigmoid).astype(BF16)
            slope[:, cols] = sigmoid * (1.0 + pre * (1.0 - sigmoid))

        one(keys, maps[span((H + head) * E, E), :], feat_k, slope_k)
        one(queries, maps[span(head * E, E), :], feat_q, slope_q)
        states[0, span(head * E, E), :] = dot(feat_k[:, cols], values[:, cols], 0, 0)

    heads(features)
    pl.semaphore_wait(barrier, plane + depth - 2)

    def chunk_copy(way, peer, chunk):
        return remote(
            states.at[way, span(peer * rows + chunk * part, part)],
            plane_in.at[way, place, pl.ds(chunk * part, part)],
            send_a.at[way, peer, chunk], recv_a.at[way, place, chunk], level, peer,
        )

    def chunk_arrival(way, peer, chunk):
        return remote(
            states.at[way, span(place * rows + chunk * part, part)],
            plane_in.at[way, peer, pl.ds(chunk * part, part)],
            send_a.at[way, place, chunk], recv_a.at[way, peer, chunk], level, peer,
        )

    def chain_copy(way, chunk):
        here = pl.ds(chunk * part, part)
        return remote(
            chain_out.at[way, here], chain_in.at[way, here],
            send_z.at[way, chunk], recv_z.at[way, chunk],
            (level + (depth - 1 if way else 1)) % depth, place,
        )

    def back_copy(way, peer, chunk):
        return remote(
            back.at[way, peer, pl.ds(chunk * part, part)],
            summed.at[way, span(place * rows + chunk * part, part)],
            send_c.at[way, peer, chunk], recv_c.at[way, place, chunk], level, peer,
        )

    def back_arrival(way, peer, chunk):
        return remote(
            back.at[way, place, pl.ds(chunk * part, part)],
            summed.at[way, span(peer * rows + chunk * part, part)],
            send_c.at[way, place, chunk], recv_c.at[way, peer, chunk], level, peer,
        )

    def scan_start(way):
        for chunk in range(CHUNKS):
            for peer in peers:
                chunk_copy(way, peer, chunk).start()
        plane_in[way, place] = states[way, span(place * rows, rows), :]

    def scan_middle(way):
        first, last = (depth - 1, 0) if way else (0, depth - 1)
        for chunk in range(CHUNKS):
            here = pl.ds(chunk * part, part)
            for peer in peers:
                chunk_arrival(way, peer, chunk).wait_recv()
            total = plane_in[way, 0, here, :]
            for member in range(1, plane):
                total = total + plane_in[way, member, here, :]

            @pl.when(level != first)
            def _():
                chain_copy(way, chunk).wait_recv()

            @pl.when(level == first)
            def _():
                chain_in[way, here, :] = jnp.zeros((part, E), F32)

            running = chain_in[way, here, :]

            @pl.when(level != last)
            def _():
                chain_out[way, here, :] = running + total
                chain_copy(way, chunk).start()

            members = range(plane)
            for member in reversed(members) if way else members:
                back[way, member, here, :] = running
                running = running + plane_in[way, member, here, :]
            for peer in peers:
                back_copy(way, peer, chunk).start()
            summed[way, span(place * rows + chunk * part, part), :] = back[way, place, here, :]

    def scan_end(way):
        for chunk in range(CHUNKS):
            for peer in peers:
                back_arrival(way, peer, chunk).wait_recv()

    def scan_drain(way):
        last = 0 if way else depth - 1
        for chunk in range(CHUNKS):
            for peer in peers:
                chunk_copy(way, peer, chunk).wait_send()
                back_copy(way, peer, chunk).wait_send()

            @pl.when(level != last)
            def _():
                chain_copy(way, chunk).wait_send()

    scan_start(0)

    def inside(head):
        cols = span(head * E, E)
        scores = masked(dot(feat_q[:, cols], feat_k[:, cols], 1, 1))
        raw_part[:, cols] = dot(scores, values[:, cols], 1, 0)

    heads(inside)
    scan_middle(0)
    scan_end(0)

    def forward(head):
        cols = span(head * E, E)
        before = summed[0, span(head * E, E), :].astype(BF16)
        raw = dot(feat_q[:, cols], before, 1, 0) + raw_part[:, cols]
        scale = lax.rsqrt(jnp.mean(raw * raw, -1, keepdims=True) + NORM_EPS)
        unit = raw * scale
        wide = gain[:, cols].astype(F32)
        attention[:, cols] = (unit * wide).astype(BF16)
        dunit = out_grad[:, cols].astype(F32) * wide
        inner = jnp.mean(dunit * unit, -1, keepdims=True)
        grad = (scale * (dunit - unit * inner)).astype(BF16)
        grad_raw[:, cols] = grad
        states[1, span(head * E, E), :] = dot(feat_q[:, cols], grad, 0, 0)

    heads(forward)
    scan_start(1)

    def grad_copy(side, which, peer):
        return remote(
            grads.at[side, span((which * plane + peer) * share, share)],
            grads_in.at[side, which, place],
            send_r.at[side, which, peer], recv_r.at[side, which, place], level, peer,
        )

    def grad_arrival(side, which, peer):
        return remote(
            grads.at[side, span((which * plane + place) * share, share)],
            grads_in.at[side, which, peer],
            send_r.at[side, which, place], recv_r.at[side, which, peer], level, peer,
        )

    def owner_copy(side, which):
        return remote(
            grads_part.at[side, which], rows_in.at[level],
            send_rz.at[side, which], recv_rz.at[level], side * half + which, place,
        )

    def owner_arrival(other):
        return remote(
            grads_part.at[0, 0], rows_in.at[other],
            send_rz.at[0, 0], recv_rz.at[other], other, place,
        )

    def map_rows(owner_level, owner_place):
        return new_maps.at[span((owner_level * plane + owner_place) * share, share)]

    def map_copy(side, other):
        return remote(
            map_rows(level, place), map_rows(level, place),
            send_g.at[other], recv_g.at[side, level - side * half], other, place,
        )

    def map_arrival(side, which):
        owner = side * half + which
        return remote(
            map_rows(owner, place), map_rows(owner, place),
            send_g.at[owner], recv_g.at[side, which], owner, place,
        )

    def spread_copy(side, which, peer):
        owner = side * half + which
        return remote(
            map_rows(owner, place), map_rows(owner, place),
            send_p.at[side, which, peer], recv_p.at[side, which, place], level, peer,
        )

    def spread_arrival(side, which, peer):
        owner = side * half + which
        return remote(
            map_rows(owner, peer), map_rows(owner, peer),
            send_p.at[side, which, place], recv_p.at[side, which, peer], level, peer,
        )

    def reduce_start(side):
        for which in range(half):
            for peer in peers:
                grad_copy(side, which, peer).start()

    def reduce_middle(side):
        for which in range(half):
            total = grads[side, span((which * plane + place) * share, share), :]
            for peer in peers:
                grad_arrival(side, which, peer).wait_recv()
                total = total + grads_in[side, which, peer]

            @pl.when(level == side * half + which)
            def _():
                rows_in[level] = total

            @pl.when(level != side * half + which)
            def _():
                grads_part[side, which] = total
                owner_copy(side, which).start()

    def update(side):
        @pl.when(level // half == side)
        def _():
            for other in levels:
                owner_arrival(other).wait_recv()
            gradient = rows_in[0]
            for other in range(1, depth):
                gradient = gradient + rows_in[other]
            mine = span(me * share, share)
            rows_new, first_new, second_new = adam_rows(
                gradient, maps[mine, :], first_old[...], second_old[...]
            )
            new_maps[mine, :] = rows_new
            new_moments[0] = first_new
            new_moments[1] = second_new
            for other in levels:
                map_copy(side, other).start()

    def spread(side):
        for which in range(half):

            @pl.when(level != side * half + which)
            def _():
                map_arrival(side, which).wait_recv()

            for peer in peers:
                spread_copy(side, which, peer).start()

    def spread_end(side):
        for which in range(half):
            for peer in peers:
                spread_arrival(side, which, peer).wait_recv()

    def drain(side):
        for which in range(half):
            for peer in peers:
                grad_copy(side, which, peer).wait_send()
                spread_copy(side, which, peer).wait_send()

            @pl.when(level != side * half + which)
            def _():
                owner_copy(side, which).wait_send()

        @pl.when(level // half == side)
        def _():
            for other in levels:
                map_copy(side, other).wait_send()

    def query_side(head):
        cols = span(head * E, E)
        grad = grad_raw[:, cols]
        pscores = masked(dot(grad, values[:, cols], 1, 1))
        before = summed[0, span(head * E, E), :].astype(BF16)
        grad_fq = dot(grad, before, 1, 1) + dot(pscores, feat_k[:, cols], 1, 0)
        local_fk[:, cols] = dot(pscores, feat_q[:, cols], 0, 0)
        grad_pq = (grad_fq * slope_q[:, cols]).astype(BF16)
        grads[0, span(head * E, E), :] = dot(queries[:, cols], grad_pq, 0, 0)

    heads(query_side)
    reduce_start(0)
    scan_middle(1)
    reduce_middle(0)
    scan_end(1)

    def key_side(head):
        cols = span(head * E, E)
        after = summed[1, span(head * E, E), :].astype(BF16)
        grad_fk = dot(values[:, cols], after, 1, 1) + local_fk[:, cols]
        grad_pk = (grad_fk * slope_k[:, cols]).astype(BF16)
        grads[1, span(head * E, E), :] = dot(keys[:, cols], grad_pk, 0, 0)

    heads(key_side)
    reduce_start(1)
    update(0)
    reduce_middle(1)
    spread(0)
    update(1)
    spread(1)
    spread_end(0)
    spread_end(1)
    scan_drain(0)
    scan_drain(1)
    drain(0)
    drain(1)


def local(count, queries, keys, values, out_grad, maps, gain, first_moment, second_moment):
    depth, plane = layout(count)
    half = depth // 2
    share = 2 * H * E // count
    rows = H * E // plane
    tokens = queries.shape[0]
    wide = (SPAN, H * E)
    dma = pltpu.SemaphoreType.DMA
    scratch = [
        pltpu.VMEM(wide, BF16),
        pltpu.VMEM(wide, BF16),
        pltpu.VMEM(wide, F32),
        pltpu.VMEM(wide, F32),
        pltpu.VMEM(wide, F32),
        pltpu.VMEM(wide, BF16),
        pltpu.VMEM(wide, F32),
        pltpu.VMEM((2, H * E, E), F32),
        pltpu.VMEM((2, plane, rows, E), F32),
        pltpu.VMEM((2, rows, E), F32),
        pltpu.VMEM((2, rows, E), F32),
        pltpu.VMEM((2, plane, rows, E), F32),
        pltpu.VMEM((2, H * E, E), F32),
        pltpu.VMEM((2, H * E, E), F32),
        pltpu.VMEM((2, half, plane, share, E), F32),
        pltpu.VMEM((2, half, share, E), F32),
        pltpu.VMEM((depth, share, E), F32),
        dma((2, plane, CHUNKS)),
        dma((2, plane, CHUNKS)),
        dma((2, CHUNKS)),
        dma((2, CHUNKS)),
        dma((2, plane, CHUNKS)),
        dma((2, plane, CHUNKS)),
        dma((2, half, plane)),
        dma((2, half, plane)),
        dma((2, half)),
        dma((depth,)),
        dma((depth,)),
        dma((2, half)),
        dma((2, half, plane)),
        dma((2, half, plane)),
    ]
    vmem = pl.BlockSpec(memory_space=pltpu.VMEM)
    attention, new_maps, new_moments = pl.pallas_call(
        functools.partial(kernel, depth, plane, share),
        out_shape=(
            jax.ShapeDtypeStruct((tokens, H * E), BF16),
            jax.ShapeDtypeStruct((2 * H * E, E), F32),
            jax.ShapeDtypeStruct((2, share, E), F32),
        ),
        in_specs=[vmem] * 8,
        out_specs=(vmem, vmem, vmem),
        scratch_shapes=scratch,
        compiler_params=pltpu.CompilerParams(
            collective_id=0, has_side_effects=True, vmem_limit_bytes=40 * 1024 * 1024
        ),
        name="layer",
    )(
        queries, keys, values, out_grad, maps.reshape(2 * H * E, E), gain.reshape(1, H * E),
        first_moment, second_moment,
    )
    return attention, new_maps.reshape(2, H, E, E), new_moments


def solution(mesh):
    in_specs = (
        P(("groups", "seq"), None),
        P(("groups", "seq"), None),
        P(("groups", "seq"), None),
        P(("groups", "seq"), None),
        P(),
        P(),
        P("seq", None),
        P("seq", None),
    )
    out_specs = (
        P(("groups", "seq"), None),
        P("groups", None, None, None),
        P("groups", "seq", None),
    )
    return jax.shard_map(
        functools.partial(local, mesh.shape["seq"]),
        mesh=mesh, in_specs=in_specs, out_specs=out_specs, check_vma=False,
    )
```

time: 326 us -> 86.6 us (0.27)
  waiting for transfers between devices: 232 us -> 0 us
  Pallas kernels: 0 us -> 75.2 us
  other arithmetic: 41.7 us -> 0 us
  matrix products: 19.2 us -> 0 us
  between operations: 14 us -> 0.65 us
  local copies, waits for them, and re-layouts: 16.3 us -> 10.2 us
    all_gather x3 -> x0, waiting for transfers between devices: 176 us -> none  [the longest x2 140 us: prefix(): pieces = lax.all_gather(value, axis)]
    pallas_call x0 -> x1, Pallas kernels: none -> 75.2 us  [local(): pl.pallas_call(functools.partial(kernel, depth, plane, share), out_shape=...]
    reduce_scatter x1 -> x0, waiting for transfers between devices: 55.7 us -> none  [local(): lax.psum_scatter(local_grad, 'seq', scatter_dimension=0, tiled=True)]
    select_n x30 -> x0, other arithmetic: 36.9 us -> none  [lap(): return jnp.where(position < mine, longer, total)]
    dot_general x11 -> x0, matrix products: 19.2 us -> none  [product(): return jnp.einsum(form, left, right, preferred_element_type=jnp.float32)]
    rev x1 -> x0, local copies, waits for them, and re-layouts: 7.71 us -> none  [prefix(): pieces = pieces[::-1]]
    unnamed x37 -> x17, local copies, waits for them, and re-layouts: 5.07 us -> 9.49 us
    another operation x4 -> x0, other arithmetic: 4.38 us -> none  [the longest x2 2.22 us: local(): return (attention, new_maps, jnp.stack([first_new, second_new]))]
  transfers between devices with their start and end apart: 4 -> 0, of which waited for: 4 -> 0; matrix products, arithmetic and copies ran while one was open for 4% -> 0% of each run, Pallas kernels for 0% -> 0%
where the time goes in v1:
time: 86.6 us; the launch traced here: 86 us
  Pallas kernels  75.2 us (87%)
  local copies, waits for them, and re-layouts  10.2 us (12%)
    pallas_call x1, Pallas kernels, local(): pl.pallas_call(functools.partial(kernel, depth, plane, share), out_shape=...  75.2 us
    unnamed x17, local copies, waits for them, and re-layouts  9.49 us

profile of v1, /device:TPU:0, one launch (start us, length us, event | category | flops | bytes accessed | tf_op | source)
XLA Modules:
  0.0 86.0 jit_solution(1787151482588074578)
XLA Ops:
  0.6 0.7 reshape.16.gain
  1.3 0.0 copy-start
  1.3 1.2 %copy-done = f32[2,8,128,128]{3,2,1,0:T(8,128)S(1)} copy-done((f32[2,8,128,128]{3,2,1,0:T(8,128)S(1)}, f32[2,8,128,128]{3,2,1,0:T(8,128)}, u32[]{:S(2)}) %copy-start) | copy-done | bytes 1048600
  2.5 0.0 copy-start.1
  2.5 1.0 %copy-done.1 = bf16[256,1024]{1,0:T(8,128)(2,1)S(1)} copy-done((bf16[256,1024]{1,0:T(8,128)(2,1)S(1)}, bf16[256,1024]{1,0:T(8,128)(2,1)}, u32[]{:S(2)}) %copy-start.1) | copy-done | bytes 524312
  3.6 0.0 copy-start.2
  3.6 1.0 %copy-done.2 = bf16[256,1024]{1,0:T(8,128)(2,1)S(1)} copy-done((bf16[256,1024]{1,0:T(8,128)(2,1)S(1)}, bf16[256,1024]{1,0:T(8,128)(2,1)}, u32[]{:S(2)}) %copy-start.2) | copy-done | bytes 524312
  4.6 0.0 copy-start.3
  4.6 1.0 %copy-done.3 = bf16[256,1024]{1,0:T(8,128)(2,1)S(1)} copy-done((bf16[256,1024]{1,0:T(8,128)(2,1)S(1)}, bf16[256,1024]{1,0:T(8,128)(2,1)}, u32[]{:S(2)}) %copy-start.3) | copy-done | bytes 524312
  5.7 0.0 copy-start.4
  5.7 1.0 %copy-done.4 = bf16[256,1024]{1,0:T(8,128)(2,1)S(1)} copy-done((bf16[256,1024]{1,0:T(8,128)(2,1)S(1)}, bf16[256,1024]{1,0:T(8,128)(2,1)}, u32[]{:S(2)}) %copy-start.4) | copy-done | bytes 524312
  6.7 0.0 copy-start.5
  6.7 0.8 copy-done.5
  7.6 0.0 copy-start.6
  7.6 0.8 copy-done.6
  8.4 75.2 %layer.1 = (bf16[256,1024]{1,0:T(8,128)(2,1)S(1)}, f32[2048,128]{1,0:T(8,128)S(1)}, f32[2,128,128]{2,1,0:T(8,128)S(1)}) custom-call(bf16[256,1024]{1,0:T(8,128)(2,1)S(1)} %copy-done.1, bf16[256,1024]{1,0:T(8,128)(2,1)S(1)} %copy-done.2, bf16[256,1024]{1,0:T(8,128)(2,1)S(1)} %copy-done.3, bf16[256,1024]{1,0:T(8,128)(2,1)S(1)} %copy-done.4, ...), custom_call_target="tpu_custom_call" | custom-call | tf_op jit(solution)/shard_map/layer/pallas_call | solution.py:444
  83.6 0.8 copy.14
  84.4 1.0 %copy.15 = f32[2,8,128,128]{3,2,1,0:T(8,128)} copy(f32[2,8,128,128]{3,2,1,0:T(8,128)S(1)} %bitcast.3) | data formatting | bytes 2097152
  85.4 0.7 copy.16
Async XLA Ops:
  1.3 1.2 %copy-start = (f32[2,8,128,128]{3,2,1,0:T(8,128)S(1)}, f32[2,8,128,128]{3,2,1,0:T(8,128)}, u32[]{:S(2)}) copy-start(f32[2,8,128,128]{3,2,1,0:T(8,128)} %param.12) | copy-start | bytes 3145732
  2.5 1.0 %copy-start.1 = (bf16[256,1024]{1,0:T(8,128)(2,1)S(1)}, bf16[256,1024]{1,0:T(8,128)(2,1)}, u32[]{:S(2)}) copy-start(bf16[256,1024]{1,0:T(8,128)(2,1)} %queries.1) | copy-start | bytes 1572868
  3.6 1.0 %copy-start.2 = (bf16[256,1024]{1,0:T(8,128)(2,1)S(1)}, bf16[256,1024]{1,0:T(8,128)(2,1)}, u32[]{:S(2)}) copy-start(bf16[256,1024]{1,0:T(8,128)(2,1)} %keys.1) | copy-start | bytes 1572868
  4.6 1.0 %copy-start.3 = (bf16[256,1024]{1,0:T(8,128)(2,1)S(1)}, bf16[256,1024]{1,0:T(8,128)(2,1)}, u32[]{:S(2)}) copy-start(bf16[256,1024]{1,0:T(8,128)(2,1)} %values.1) | copy-start | bytes 1572868
  5.7 1.0 %copy-start.4 = (bf16[256,1024]{1,0:T(8,128)(2,1)S(1)}, bf16[256,1024]{1,0:T(8,128)(2,1)}, u32[]{:S(2)}) copy-start(bf16[256,1024]{1,0:T(8,128)(2,1)} %out_grad.1) | copy-start | bytes 1572868
  6.7 0.8 copy-start.5
  7.6 0.8 copy-start.6

commit v2 on v1

v2 whole, which is shorter than its diff:
```python
import functools

import jax
import jax.numpy as jnp
from jax import lax
from jax.experimental import pallas as pl
from jax.experimental.pallas import tpu as pltpu
from jax.sharding import PartitionSpec as P

H = 8
E = 128
SPAN = 256
OPT_STEP = 10
PAIRS = 4

BETA_ONE = 0.9
BETA_TWO = 0.95
RATE = 0.01
TINY = 1e-08
NORM_EPS = 1e-06

F32 = jnp.float32
BF16 = jnp.bfloat16


def dot(left, right, left_dim, right_dim):
    return lax.dot_general(
        left, right, (((left_dim,), (right_dim,)), ((), ())), preferred_element_type=F32
    )


def adam_rows(gradient, weights, first_old, second_old):
    first_new = BETA_ONE * first_old + (1.0 - BETA_ONE) * gradient
    second_new = BETA_TWO * second_old + (1.0 - BETA_TWO) * gradient * gradient
    first_hat = first_new / (1.0 - BETA_ONE**OPT_STEP)
    second_hat = second_new / (1.0 - BETA_TWO**OPT_STEP)
    return (weights - RATE * first_hat / (jnp.sqrt(second_hat) + TINY), first_new, second_new)


def layout(count):
    chips = count // 2
    row = 1
    while row * row * 4 <= chips:
        row *= 2
    return chips // row, row


def kernel(
    depth, width, share,
    queries_hbm, keys_hbm, values_hbm, out_grad_hbm, maps_hbm, first_hbm, second_hbm, gain,
    attention, new_maps, new_moments,
    queries, keys, values, out_grad, maps, first_old, second_old,
    feat_q, feat_k, slope_q, slope_k, raw_part, grad_raw, local_fk,
    states, core_in, chip, row_in, chain_in, chain_out, share_out, summed,
    grads, grads_core, grads_chip, grads_row, grads_part, rows_in,
    load,
    send_core, recv_core, send_row, recv_row, send_z, recv_z, send_share, recv_share,
    send_rc, recv_rc, send_ry, recv_ry, send_rz, recv_rz,
    send_gz, recv_gz, send_gy, recv_gy, send_gc, recv_gc,
):
    group = lax.axis_index("groups")
    me = lax.axis_index("seq")
    plane = 2 * width
    level = me // plane
    row = (me // 2) % width
    core = me % 2
    other_core = 1 - core
    half = depth // 2
    chunks = half * width
    per_pair = chunks // PAIRS
    rows_beside = [(row + step) % width for step in range(1, width)]
    levels = [(level + step) % depth for step in range(1, depth)]

    def index(to_level, to_row, to_core):
        return to_level * plane + to_row * 2 + to_core

    def remote(src, dst, send, recv, to_level, to_row, to_core):
        return pltpu.make_async_remote_copy(
            src_ref=src, dst_ref=dst, send_sem=send, recv_sem=recv,
            device_id=(group, index(to_level, to_row, to_core)),
            device_id_type=pl.DeviceIdType.MESH,
        )

    def span(start, size):
        return pl.ds(pl.multiple_of(start, size), size)

    def head_rows(head):
        return span(head * E, E)

    def greet(to):
        pl.semaphore_signal(
            barrier, inc=1, device_id=(group, to), device_id_type=pl.DeviceIdType.MESH
        )

    loads = [
        pltpu.make_async_copy(src, dst, load.at[slot])
        for slot, (src, dst) in enumerate(
            (
                (keys_hbm, keys),
                (maps_hbm, maps),
                (values_hbm, values),
                (queries_hbm, queries),
                (out_grad_hbm, out_grad),
                (first_hbm, first_old),
                (second_hbm, second_old),
            )
        )
    ]
    for one in loads:
        one.start()

    barrier = pltpu.get_barrier_semaphore()
    greet(index(level, row, other_core))
    for beside in rows_beside:
        greet(index(level, beside, core))
    for other in levels:
        greet(index(other, row, core))

    def masked(scores):
        line = lax.broadcasted_iota(jnp.int32, (SPAN, SPAN), 0)
        column = lax.broadcasted_iota(jnp.int32, (SPAN, SPAN), 1)
        return jnp.where(line >= column, scores, 0.0).astype(BF16)

    def both(body, pair):
        body(2 * pair)
        body(2 * pair + 1)

    def core_copy(way, pair):
        return remote(
            states.at[way, head_rows(2 * pair + other_core)], core_in.at[way, pair],
            send_core.at[way, pair], recv_core.at[way, pair], level, row, other_core,
        )

    def row_copy(way, pair, beside):
        return remote(
            chip.at[way, pair], row_in.at[way, row, pair],
            send_row.at[way, beside, pair], recv_row.at[way, row, pair], level, beside, core,
        )

    def row_arrival(way, pair, beside):
        return remote(
            chip.at[way, pair], row_in.at[way, beside, pair],
            send_row.at[way, row, pair], recv_row.at[way, beside, pair], level, beside, core,
        )

    def chain_copy(way, pair):
        return remote(
            chain_out.at[way, pair], chain_in.at[way, pair],
            send_z.at[way, pair], recv_z.at[way, pair],
            (level + (depth - 1 if way else 1)) % depth, row, core,
        )

    def share_copy(way, pair):
        mine = head_rows(2 * pair + core)
        return remote(
            share_out.at[way, pair], summed.at[way, mine],
            send_share.at[way, pair], recv_share.at[way, pair], level, row, other_core,
        )

    def share_arrival(way, pair):
        theirs = head_rows(2 * pair + other_core)
        return remote(
            share_out.at[way, pair], summed.at[way, theirs],
            send_share.at[way, pair], recv_share.at[way, pair], level, row, other_core,
        )

    def scan_rows(way, pair):
        core_copy(way, pair).wait_recv()
        own = states[way, head_rows(2 * pair + core), :]
        total = own + core_in[way, pair]
        chip[way, pair] = total
        for beside in rows_beside:
            row_copy(way, pair, beside).start()
        row_in[way, row, pair] = total

    def scan_levels(way, pair, first):
        last = 0 if way else depth - 1

        def steps():
            for beside in rows_beside:
                row_arrival(way, pair, beside).wait_recv()
            ahead = jnp.zeros((E, E), F32)
            total = jnp.zeros((E, E), F32)
            for member in range(width):
                one = row_in[way, member, pair]
                total = total + one
                counts = (member > row) if way else (member < row)
                ahead = ahead + jnp.where(counts, one, 0.0)
            if first:
                chain_out[way, pair] = total
                chain_copy(way, pair).start()
            else:
                chain_copy(way, pair).wait_recv()
                running = chain_in[way, pair]
                ahead = ahead + running

                @pl.when(level != last)
                def _():
                    chain_out[way, pair] = running + total
                    chain_copy(way, pair).start()

            near = core == (1 if way else 0)
            mine = head_rows(2 * pair + core)
            share_out[way, pair] = ahead + jnp.where(near, states[way, mine, :], 0.0)
            share_copy(way, pair).start()
            summed[way, mine, :] = ahead + jnp.where(near, 0.0, core_in[way, pair])

        at_first = level == (depth - 1 if way else 0)
        pl.when(at_first if first else jnp.logical_not(at_first))(steps)

    def scan_drain(way):
        last = 0 if way else depth - 1
        for pair in range(PAIRS):
            core_copy(way, pair).wait_send()
            share_copy(way, pair).wait_send()
            for beside in rows_beside:
                row_copy(way, pair, beside).wait_send()

            @pl.when(level != last)
            def _():
                chain_copy(way, pair).wait_send()

    def piece(chunk, of_core):
        return span((chunk * 2 + of_core) * share, share)

    def reduce_core_copy(side, chunk):
        return remote(
            grads.at[side, piece(chunk, other_core)], grads_core.at[side, chunk],
            send_rc.at[side, chunk], recv_rc.at[side, chunk], level, row, other_core,
        )

    def reduce_row_copy(side, chunk):
        which, to_row = chunk // width, chunk % width
        return remote(
            grads_chip.at[side, chunk], grads_row.at[side, which, row],
            send_ry.at[side, chunk], recv_ry.at[side, which, row], level, to_row, core,
        )

    def reduce_row_arrival(side, which, beside):
        return remote(
            grads_chip.at[side, 0], grads_row.at[side, which, beside],
            send_ry.at[side, 0], recv_ry.at[side, which, beside], level, beside, core,
        )

    def owner_copy(side, which):
        return remote(
            grads_part.at[side, which], rows_in.at[level],
            send_rz.at[side, which], recv_rz.at[level], side * half + which, row, core,
        )

    def owner_arrival(other):
        return remote(
            grads_part.at[0, 0], rows_in.at[other],
            send_rz.at[0, 0], recv_rz.at[other], other, row, core,
        )

    def reduce_start(side, pair):
        for chunk in range(pair * per_pair, (pair + 1) * per_pair):
            reduce_core_copy(side, chunk).start()

    def reduce_rows(side, pair):
        for chunk in range(pair * per_pair, (pair + 1) * per_pair):
            which, to_row = chunk // width, chunk % width
            reduce_core_copy(side, chunk).wait_recv()
            total = grads[side, piece(chunk, core), :] + grads_core[side, chunk]

            @pl.when(row == to_row)
            def _():
                grads_row[side, which, row] = total

            @pl.when(row != to_row)
            def _():
                grads_chip[side, chunk] = total
                reduce_row_copy(side, chunk).start()

    def reduce_levels(side, which):
        for beside in rows_beside:
            reduce_row_arrival(side, which, beside).wait_recv()
        total = grads_row[side, which, 0]
        for member in range(1, width):
            total = total + grads_row[side, which, member]

        @pl.when(level == side * half + which)
        def _():
            rows_in[level] = total

        @pl.when(level != side * half + which)
        def _():
            grads_part[side, which] = total
            owner_copy(side, which).start()

    def map_rows(of_level, of_row, of_core):
        return new_maps.at[span(index(of_level, of_row, of_core) * share, share)]

    def map_level_copy(side, other):
        mine = map_rows(level, row, core)
        return remote(
            mine, mine, send_gz.at[other], recv_gz.at[side, level - side * half],
            other, row, core,
        )

    def map_level_arrival(side, which):
        owner = side * half + which
        theirs = map_rows(owner, row, core)
        return remote(
            theirs, theirs, send_gz.at[owner], recv_gz.at[side, which], owner, row, core
        )

    def map_row_copy(side, which, beside):
        mine = map_rows(side * half + which, row, core)
        return remote(
            mine, mine, send_gy.at[side, which, beside], recv_gy.at[side, which, row],
            level, beside, core,
        )

    def map_row_arrival(side, which, beside):
        theirs = map_rows(side * half + which, beside, core)
        return remote(
            theirs, theirs, send_gy.at[side, which, row], recv_gy.at[side, which, beside],
            level, beside, core,
        )

    def map_core_copy(side, which, of_row):
        mine = map_rows(side * half + which, of_row, core)
        return remote(
            mine, mine, send_gc.at[side, which, of_row], recv_gc.at[side, which, of_row],
            level, row, other_core,
        )

    def map_core_arrival(side, which, of_row):
        theirs = map_rows(side * half + which, of_row, other_core)
        return remote(
            theirs, theirs, send_gc.at[side, which, of_row], recv_gc.at[side, which, of_row],
            level, row, other_core,
        )

    def update(side):
        @pl.when(level // half == side)
        def _():
            for other in levels:
                owner_arrival(other).wait_recv()
            gradient = rows_in[0]
            for other in range(1, depth):
                gradient = gradient + rows_in[other]
            mine = span(me * share, share)
            rows_new, first_new, second_new = adam_rows(
                gradient, maps[mine, :], first_old[...], second_old[...]
            )
            new_maps[mine, :] = rows_new
            for other in levels:
                map_level_copy(side, other).start()
            new_moments[0] = first_new
            new_moments[1] = second_new

    def spread(side):
        for which in range(half):

            @pl.when(level != side * half + which)
            def _():
                map_level_arrival(side, which).wait_recv()

            for beside in rows_beside:
                map_row_copy(side, which, beside).start()
            map_core_copy(side, which, row).start()

    def spread_core(side):
        for which in range(half):
            for beside in rows_beside:
                map_row_arrival(side, which, beside).wait_recv()
                map_core_copy(side, which, beside).start()

    def spread_end(side):
        for which in range(half):
            for of_row in range(width):
                map_core_arrival(side, which, of_row).wait_recv()

    def drain(side):
        for chunk in range(chunks):
            reduce_core_copy(side, chunk).wait_send()

            @pl.when(row != chunk % width)
            def _():
                reduce_row_copy(side, chunk).wait_send()

        for which in range(half):
            for beside in rows_beside:
                map_row_copy(side, which, beside).wait_send()
            for of_row in range(width):
                map_core_copy(side, which, of_row).wait_send()

            @pl.when(level != side * half + which)
            def _():
                owner_copy(side, which).wait_send()

        @pl.when(level // half == side)
        def _():
            for other in levels:
                map_level_copy(side, other).wait_send()

    def feature(source, weights, feat, slope, cols):
        pre = dot(source[:, cols], weights.astype(BF16), 1, 0)
        sigmoid = 1.0 / (1.0 + jnp.exp(-pre))
        feat[:, cols] = (pre * sigmoid).astype(BF16)
        slope[:, cols] = sigmoid * (1.0 + pre * (1.0 - sigmoid))

    def key_features(head):
        cols = head_rows(head)
        feature(keys, maps[head_rows(H + head), :], feat_k, slope_k, cols)
        states[0, head_rows(head), :] = dot(feat_k[:, cols], values[:, cols], 0, 0)

    def query_features(head):
        cols = head_rows(head)
        feature(queries, maps[head_rows(head), :], feat_q, slope_q, cols)

    def inside(head):
        cols = head_rows(head)
        scores = masked(dot(feat_q[:, cols], feat_k[:, cols], 1, 1))
        raw_part[:, cols] = dot(scores, values[:, cols], 1, 0)

    def forward(head):
        cols = head_rows(head)
        before = summed[0, head_rows(head), :].astype(BF16)
        raw = dot(feat_q[:, cols], before, 1, 0) + raw_part[:, cols]
        scale = lax.rsqrt(jnp.mean(raw * raw, -1, keepdims=True) + NORM_EPS)
        unit = raw * scale
        wide = gain[:, cols].astype(F32)
        attention[:, cols] = (unit * wide).astype(BF16)
        dunit = out_grad[:, cols].astype(F32) * wide
        inner = jnp.mean(dunit * unit, -1, keepdims=True)
        grad = (scale * (dunit - unit * inner)).astype(BF16)
        grad_raw[:, cols] = grad
        states[1, head_rows(head), :] = dot(feat_q[:, cols], grad, 0, 0)

    def query_side(head):
        cols = head_rows(head)
        grad = grad_raw[:, cols]
        pscores = masked(dot(grad, values[:, cols], 1, 1))
        before = summed[0, head_rows(head), :].astype(BF16)
        grad_fq = dot(grad, before, 1, 1) + dot(pscores, feat_k[:, cols], 1, 0)
        local_fk[:, cols] = dot(pscores, feat_q[:, cols], 0, 0)
        grad_pq = (grad_fq * slope_q[:, cols]).astype(BF16)
        grads[0, head_rows(head), :] = dot(queries[:, cols], grad_pq, 0, 0)

    def key_side(head):
        cols = head_rows(head)
        after = summed[1, head_rows(head), :].astype(BF16)
        grad_fk = dot(values[:, cols], after, 1, 1) + local_fk[:, cols]
        grad_pk = (grad_fk * slope_k[:, cols]).astype(BF16)
        grads[1, head_rows(head), :] = dot(keys[:, cols], grad_pk, 0, 0)

    def keys_pair(pair):
        both(key_features, pair)
        if pair == 0:
            pl.semaphore_wait(barrier, 1 + width - 1 + depth - 1)
        core_copy(0, pair).start()

    def forward_pair(pair):
        share_arrival(0, pair).wait_recv()
        both(forward, pair)
        core_copy(1, pair).start()

    def query_pair(pair):
        both(query_side, pair)
        reduce_start(0, pair)

    def key_pair(pair):
        share_arrival(1, pair).wait_recv()
        both(key_side, pair)
        reduce_start(1, pair)

    for one in loads[:3]:
        one.wait()
    keys_pair(0)
    keys_pair(1)
    scan_rows(0, 0)
    keys_pair(2)
    scan_rows(0, 1)
    keys_pair(3)
    scan_rows(0, 2)
    for one in loads[3:]:
        one.wait()
    both(query_features, 0)
    scan_rows(0, 3)
    both(query_features, 1)
    scan_levels(0, 0, True)
    both(query_features, 2)
    scan_levels(0, 1, True)
    both(query_features, 3)
    scan_levels(0, 2, True)
    both(inside, 0)
    scan_levels(0, 3, True)
    both(inside, 1)
    scan_levels(0, 0, False)
    both(inside, 2)
    scan_levels(0, 1, False)
    both(inside, 3)
    scan_levels(0, 2, False)
    forward_pair(0)
    scan_levels(0, 3, False)
    forward_pair(1)
    scan_rows(1, 0)
    forward_pair(2)
    scan_rows(1, 1)
    forward_pair(3)
    scan_rows(1, 2)
    query_pair(0)
    scan_rows(1, 3)
    scan_levels(1, 0, True)
    query_pair(1)
    scan_levels(1, 1, True)
    query_pair(2)
    scan_levels(1, 2, True)
    query_pair(3)
    scan_levels(1, 3, True)
    for pair in range(PAIRS):
        reduce_rows(0, pair)
    scan_levels(1, 0, False)
    scan_levels(1, 1, False)
    for which in range(half):
        reduce_levels(0, which)
    scan_levels(1, 2, False)
    key_pair(0)
    scan_levels(1, 3, False)
    key_pair(1)
    reduce_rows(1, 0)
    key_pair(2)
    reduce_rows(1, 1)
    key_pair(3)
    reduce_rows(1, 2)
    reduce_rows(1, 3)
    update(0)
    for which in range(half):
        reduce_levels(1, which)
    spread(0)
    update(1)
    spread_core(0)
    spread(1)
    spread_core(1)
    spread_end(0)
    spread_end(1)
    scan_drain(0)
    scan_drain(1)
    drain(0)
    drain(1)


def local(count, queries, keys, values, out_grad, maps, gain, first_moment, second_moment):
    depth, width = layout(count)
    half = depth // 2
    share = 2 * H * E // count
    tokens = queries.shape[0]
    wide = (SPAN, H * E)
    flat = (2 * H * E, E)
    square = (2, PAIRS, E, E)
    dma = pltpu.SemaphoreType.DMA
    chunks = half * width
    scratch = [
        pltpu.VMEM(wide, BF16),
        pltpu.VMEM(wide, BF16),
        pltpu.VMEM(wide, BF16),
        pltpu.VMEM(wide, BF16),
        pltpu.VMEM(flat, F32),
        pltpu.VMEM((share, E), F32),
        pltpu.VMEM((share, E), F32),
        pltpu.VMEM(wide, BF16),
        pltpu.VMEM(wide, BF16),
        pltpu.VMEM(wide, F32),
        pltpu.VMEM(wide, F32),
        pltpu.VMEM(wide, F32),
        pltpu.VMEM(wide, BF16),
        pltpu.VMEM(wide, F32),
        pltpu.VMEM((2, H * E, E), F32),
        pltpu.VMEM(square, F32),
        pltpu.VMEM(square, F32),
        pltpu.VMEM((2, width, PAIRS, E, E), F32),
        pltpu.VMEM(square, F32),
        pltpu.VMEM(square, F32),
        pltpu.VMEM(square, F32),
        pltpu.VMEM((2, H * E, E), F32),
        pltpu.VMEM((2, H * E, E), F32),
        pltpu.VMEM((2, chunks, share, E), F32),
        pltpu.VMEM((2, chunks, share, E), F32),
        pltpu.VMEM((2, half, width, share, E), F32),
        pltpu.VMEM((2, half, share, E), F32),
        pltpu.VMEM((depth, share, E), F32),
        dma((7,)),
        dma((2, PAIRS)),
        dma((2, PAIRS)),
        dma((2, width, PAIRS)),
        dma((2, width, PAIRS)),
        dma((2, PAIRS)),
        dma((2, PAIRS)),
        dma((2, PAIRS)),
        dma((2, PAIRS)),
        dma((2, chunks)),
        dma((2, chunks)),
        dma((2, chunks)),
        dma((2, half, width)),
        dma((2, half)),
        dma((depth,)),
        dma((depth,)),
        dma((2, half)),
        dma((2, half, width)),
        dma((2, half, width)),
        dma((2, half, width)),
        dma((2, half, width)),
    ]
    vmem = pl.BlockSpec(memory_space=pltpu.VMEM)
    anywhere = pl.BlockSpec(memory_space=pl.ANY)
    attention, new_maps, new_moments = pl.pallas_call(
        functools.partial(kernel, depth, width, share),
        out_shape=(
            jax.ShapeDtypeStruct((tokens, H * E), BF16),
            jax.ShapeDtypeStruct(flat, F32),
            jax.ShapeDtypeStruct((2, share, E), F32),
        ),
        in_specs=[anywhere] * 7 + [vmem],
        out_specs=(vmem, vmem, vmem),
        scratch_shapes=scratch,
        compiler_params=pltpu.CompilerParams(
            collective_id=0, has_side_effects=True, vmem_limit_bytes=60 * 1024 * 1024
        ),
        name="layer",
    )(
        queries, keys, values, out_grad, maps.reshape(flat),
        first_moment, second_moment, gain.reshape(1, H * E),
    )
    return attention, new_maps.reshape(2, H, E, E), new_moments


def solution(mesh):
    in_specs = (
        P(("groups", "seq"), None),
        P(("groups", "seq"), None),
        P(("groups", "seq"), None),
        P(("groups", "seq"), None),
        P(),
        P(),
        P("seq", None),
        P("seq", None),
    )
    out_specs = (
        P(("groups", "seq"), None),
        P("groups", None, None, None),
        P("groups", "seq", None),
    )
    return jax.shard_map(
        functools.partial(local, mesh.shape["seq"]),
        mesh=mesh, in_specs=in_specs, out_specs=out_specs, check_vma=False,
    )
```

time: 86.6 us -> 79.3 us (0.916)
  local copies, waits for them, and re-layouts: 10.2 us -> 4.92 us
  Pallas kernels: 75.2 us -> 73.5 us
    unnamed x17 -> x7, local copies, waits for them, and re-layouts: 9.49 us -> 3.64 us
    pallas_call x1, Pallas kernels: 75.2 us -> 73.5 us  [local(): pl.pallas_call(functools.partial(kernel, depth, width, share), out_shape=...]
where the time goes in v2:
time: 79.3 us; the launch traced here: 79.1 us
  Pallas kernels  73.5 us (93%)
  local copies, waits for them, and re-layouts  4.92 us (6%)
    pallas_call x1, Pallas kernels, local(): pl.pallas_call(functools.partial(kernel, depth, width, share), out_shape=...  73.5 us
    unnamed x7, local copies, waits for them, and re-layouts  3.64 us

profile of v2, /device:TPU:0, one launch (start us, length us, event | category | flops | bytes accessed | tf_op | source)
XLA Modules:
  0.0 79.1 jit_solution(7307606265057443479)
XLA Ops:
  0.6 1.3 %reshape.16.gain = bf16[1,1024]{1,0:T(2,128)(2,1)} reshape(bf16[1024]{0:T(1024)(128)(2,1)} %param.13) | data formatting | bytes 4096 | tf_op jit(solution)/shard_map/reshape | solution.py:626
  1.9 73.5 %layer.1 = (bf16[256,1024]{1,0:T(8,128)(2,1)}, f32[2048,128]{1,0:T(8,128)}, f32[2,128,128]{2,1,0:T(8,128)}) custom-call(bf16[256,1024]{1,0:T(8,128)(2,1)} %queries_hbm.1, bf16[256,1024]{1,0:T(8,128)(2,1)} %keys_hbm.1, bf16[256,1024]{1,0:T(8,128)(2,1)} %values_hbm.1, bf16[256,1024]{1,0:T(8,128)(2,1)} %out_grad_hbm.1, f32[2048,128]{1,0:T(8,128)} %bitcast.2, ...), custom_call_target="tpu_custom_call" | custom-call | tf_op jit(solution)/shard_map/layer/pallas_call | solution.py:610
  75.4 0.0 copy-start
  75.4 2.0 %copy.14 = bf16[256,1024]{1,0:T(8,128)(2,1)} copy(bf16[256,1024]{1,0:T(8,128)(2,1)} %get-tuple-element.12) | data formatting | bytes 1048576
  77.4 0.0 copy-done
  77.4 0.0 copy-start.1
  77.4 1.0 %copy.15 = f32[2,8,128,128]{3,2,1,0:T(8,128)} copy(f32[2,8,128,128]{3,2,1,0:T(8,128)S(1)} %bitcast.3) | data formatting | bytes 2097152
  78.4 0.1 copy-done.1
  78.4 0.7 copy.16
Async XLA Ops:
  75.4 2.0 %copy-start = (f32[2048,128]{1,0:T(8,128)S(1)}, f32[2048,128]{1,0:T(8,128)}, u32[]{:S(2)}) copy-start(f32[2048,128]{1,0:T(8,128)} %get-tuple-element.7) | copy-start | bytes 3145732
  77.4 1.0 %copy-start.1 = (f32[2,128,128]{2,1,0:T(8,128)S(1)}, f32[2,128,128]{2,1,0:T(8,128)}, u32[]{:S(2)}) copy-start(f32[2,128,128]{2,1,0:T(8,128)} %get-tuple-element.14) | copy-start | bytes 393220

commit v3 on v2

--- a/solution.py
+++ b/solution.py
@@ -48,12 +48,13 @@
 def kernel(
     depth, width, share,
     queries_hbm, keys_hbm, values_hbm, out_grad_hbm, maps_hbm, first_hbm, second_hbm, gain,
-    attention, new_maps, new_moments,
+    attention_hbm, new_maps, new_moments,
     queries, keys, values, out_grad, maps, first_old, second_old,
+    gain_row, attention, turned_q, turned_k, turned_fq,
     feat_q, feat_k, slope_q, slope_k, raw_part, grad_raw, local_fk,
     states, core_in, chip, row_in, chain_in, chain_out, share_out, summed,
     grads, grads_core, grads_chip, grads_row, grads_part, rows_in,
-    load,
+    load, store,
     send_core, recv_core, send_row, recv_row, send_z, recv_z, send_share, recv_share,
     send_rc, recv_rc, send_ry, recv_ry, send_rz, recv_rz,
     send_gz, recv_gz, send_gy, recv_gy, send_gc, recv_gc,
@@ -116,10 +117,11 @@
     for other in levels:
         greet(index(other, row, core))
 
-    def masked(scores):
+    def masked(scores, turned=False):
         line = lax.broadcasted_iota(jnp.int32, (SPAN, SPAN), 0)
         column = lax.broadcasted_iota(jnp.int32, (SPAN, SPAN), 1)
-        return jnp.where(line >= column, scores, 0.0).astype(BF16)
+        kept = (line <= column) if turned else (line >= column)
+        return jnp.where(kept, scores, 0.0).astype(BF16)
 
     def both(body, pair):
         body(2 * pair)
@@ -411,11 +413,14 @@
     def query_features(head):
         cols = head_rows(head)
         feature(queries, maps[head_rows(head), :], feat_q, slope_q, cols)
+        turned_fq[head_rows(head), :] = feat_q[:, cols].T
 
     def inside(head):
         cols = head_rows(head)
         scores = masked(dot(feat_q[:, cols], feat_k[:, cols], 1, 1))
         raw_part[:, cols] = dot(scores, values[:, cols], 1, 0)
+        turned_q[head_rows(head), :] = queries[:, cols].T
+        turned_k[head_rows(head), :] = keys[:, cols].T
 
     def forward(head):
         cols = head_rows(head)
@@ -423,13 +428,13 @@
         raw = dot(feat_q[:, cols], before, 1, 0) + raw_part[:, cols]
         scale = lax.rsqrt(jnp.mean(raw * raw, -1, keepdims=True) + NORM_EPS)
         unit = raw * scale
-        wide = gain[:, cols].astype(F32)
+        wide = gain_row[:, cols]
         attention[:, cols] = (unit * wide).astype(BF16)
         dunit = out_grad[:, cols].astype(F32) * wide
         inner = jnp.mean(dunit * unit, -1, keepdims=True)
         grad = (scale * (dunit - unit * inner)).astype(BF16)
         grad_raw[:, cols] = grad
-        states[1, head_rows(head), :] = dot(feat_q[:, cols], grad, 0, 0)
+        states[1, head_rows(head), :] = dot(turned_fq[head_rows(head), :], grad, 1, 0)
 
     def query_side(head):
         cols = head_rows(head)
@@ -437,16 +442,17 @@
         pscores = masked(dot(grad, values[:, cols], 1, 1))
         before = summed[0, head_rows(head), :].astype(BF16)
         grad_fq = dot(grad, before, 1, 1) + dot(pscores, feat_k[:, cols], 1, 0)
-        local_fk[:, cols] = dot(pscores, feat_q[:, cols], 0, 0)
+        turned = masked(dot(values[:, cols], grad, 1, 1), True)
+        local_fk[:, cols] = dot(turned, feat_q[:, cols], 1, 0)
         grad_pq = (grad_fq * slope_q[:, cols]).astype(BF16)
-        grads[0, head_rows(head), :] = dot(queries[:, cols], grad_pq, 0, 0)
+        grads[0, head_rows(head), :] = dot(turned_q[head_rows(head), :], grad_pq, 1, 0)
 
     def key_side(head):
         cols = head_rows(head)
         after = summed[1, head_rows(head), :].astype(BF16)
         grad_fk = dot(values[:, cols], after, 1, 1) + local_fk[:, cols]
         grad_pk = (grad_fk * slope_k[:, cols]).astype(BF16)
-        grads[1, head_rows(head), :] = dot(keys[:, cols], grad_pk, 0, 0)
+        grads[1, head_rows(head), :] = dot(turned_k[head_rows(head), :], grad_pk, 1, 0)
 
     def keys_pair(pair):
         both(key_features, pair)
@@ -479,6 +485,7 @@
     scan_rows(0, 2)
     for one in loads[3:]:
         one.wait()
+    gain_row[...] = gain[...].astype(F32).reshape(1, H * E)
     both(query_features, 0)
     scan_rows(0, 3)
     both(query_features, 1)
@@ -501,34 +508,40 @@
     scan_rows(1, 0)
     forward_pair(2)
     scan_rows(1, 1)
+    scan_levels(1, 0, True)
     forward_pair(3)
+    leave = pltpu.make_async_copy(attention, attention_hbm, store)
+    leave.start()
     scan_rows(1, 2)
+    scan_levels(1, 1, True)
     query_pair(0)
     scan_rows(1, 3)
-    scan_levels(1, 0, True)
+    scan_levels(1, 2, True)
     query_pair(1)
-    scan_levels(1, 1, True)
+    scan_levels(1, 3, True)
+    reduce_rows(0, 0)
     query_pair(2)
-    scan_levels(1, 2, True)
+    reduce_rows(0, 1)
     query_pair(3)
-    scan_levels(1, 3, True)
-    for pair in range(PAIRS):
-        reduce_rows(0, pair)
     scan_levels(1, 0, False)
+    reduce_rows(0, 2)
+    reduce_rows(0, 3)
     scan_levels(1, 1, False)
-    for which in range(half):
+    for which in range(half // 2):
         reduce_levels(0, which)
     scan_levels(1, 2, False)
+    for which in range(half // 2, half):
+        reduce_levels(0, which)
     key_pair(0)
     scan_levels(1, 3, False)
     key_pair(1)
     reduce_rows(1, 0)
+    update(0)
     key_pair(2)
     reduce_rows(1, 1)
     key_pair(3)
     reduce_rows(1, 2)
     reduce_rows(1, 3)
-    update(0)
     for which in range(half):
         reduce_levels(1, which)
     spread(0)
@@ -542,6 +555,15 @@
     scan_drain(1)
     drain(0)
     drain(1)
+    leave.wait()
+
+
+def hand_over(*refs):
+    copies = [pltpu.make_async_copy(refs[i], refs[3 + i], refs[6].at[i]) for i in range(3)]
+    for one in copies:
+        one.start()
+    for one in copies:
+        one.wait()
 
 
 def local(count, queries, keys, values, out_grad, maps, gain, first_moment, second_moment):
@@ -554,6 +576,7 @@
     square = (2, PAIRS, E, E)
     dma = pltpu.SemaphoreType.DMA
     chunks = half * width
+    turned = (H * E, SPAN)
     scratch = [
         pltpu.VMEM(wide, BF16),
         pltpu.VMEM(wide, BF16),
@@ -562,6 +585,11 @@
         pltpu.VMEM(flat, F32),
         pltpu.VMEM((share, E), F32),
         pltpu.VMEM((share, E), F32),
+        pltpu.VMEM((1, H * E), F32),
+        pltpu.VMEM(wide, BF16),
+        pltpu.VMEM(turned, BF16),
+        pltpu.VMEM(turned, BF16),
+        pltpu.VMEM(turned, BF16),
         pltpu.VMEM(wide, BF16),
         pltpu.VMEM(wide, BF16),
         pltpu.VMEM(wide, F32),
@@ -584,6 +612,7 @@
         pltpu.VMEM((2, half, share, E), F32),
         pltpu.VMEM((depth, share, E), F32),
         dma((7,)),
+        dma,
         dma((2, PAIRS)),
         dma((2, PAIRS)),
         dma((2, width, PAIRS)),
@@ -615,7 +644,7 @@
             jax.ShapeDtypeStruct((2, share, E), F32),
         ),
         in_specs=[anywhere] * 7 + [vmem],
-        out_specs=(vmem, vmem, vmem),
+        out_specs=(anywhere, vmem, vmem),
         scratch_shapes=scratch,
         compiler_params=pltpu.CompilerParams(
             collective_id=0, has_side_effects=True, vmem_limit_bytes=60 * 1024 * 1024
@@ -623,8 +652,18 @@
         name="layer",
     )(
         queries, keys, values, out_grad, maps.reshape(flat),
-        first_moment, second_moment, gain.reshape(1, H * E),
+        first_moment, second_moment, gain,
     )
+    results = (attention, new_maps, new_moments)
+    attention, new_maps, new_moments = pl.pallas_call(
+        hand_over,
+        out_shape=tuple(jax.ShapeDtypeStruct(one.shape, one.dtype) for one in results),
+        in_specs=[anywhere] * 3,
+        out_specs=(anywhere,) * 3,
+        scratch_shapes=[dma((3,))],
+        compiler_params=pltpu.CompilerParams(vmem_limit_bytes=63 * 1024 * 1024),
+        name="results",
+    )(*results)
     return attention, new_maps.reshape(2, H, E, E), new_moments
 
 

time: 79.3 us -> 128 us (1.61)
  Pallas kernels: 73.5 us -> 126 us
  local copies, waits for them, and re-layouts: 4.92 us -> 0 us
    pallas_call x0 -> x1, Pallas kernels: none -> 52.7 us  [local(): pl.pallas_call(hand_over, out_shape=tuple((jax.ShapeDtypeStruct(one.shape...]
    unnamed x7 -> x0, local copies, waits for them, and re-layouts: 3.64 us -> none
where the time goes in v3:
time: 128 us; the launch traced here: 127 us
  Pallas kernels  126 us (98%)
    pallas_call x1, Pallas kernels, local(): pl.pallas_call(functools.partial(kernel, depth, width, share), out_shape=...  73.6 us
    pallas_call x1, Pallas kernels, local(): pl.pallas_call(hand_over, out_shape=tuple((jax.ShapeDtypeStruct(one.shape...  52.7 us

profile of v3, /device:TPU:0, one launch (start us, length us, event | category | flops | bytes accessed | tf_op | source)
XLA Modules:
  0.0 127.0 jit_solution(4281859636510916448)
XLA Ops:
  0.6 73.6 %layer.1 = (bf16[256,1024]{1,0:T(8,128)(2,1)}, f32[2048,128]{1,0:T(8,128)}, f32[2,128,128]{2,1,0:T(8,128)}) custom-call(bf16[256,1024]{1,0:T(8,128)(2,1)} %queries_hbm.1, bf16[256,1024]{1,0:T(8,128)(2,1)} %keys_hbm.1, bf16[256,1024]{1,0:T(8,128)(2,1)} %values_hbm.1, bf16[256,1024]{1,0:T(8,128)(2,1)} %out_grad_hbm.1, f32[2048,128]{1,0:T(8,128)} %bitcast.2, ...), custom_call_target="tpu_custom_call" | custom-call | tf_op jit(solution)/shard_map/layer/pallas_call | solution.py:639
  74.2 52.7 %results.1 = (bf16[256,1024]{1,0:T(8,128)(2,1)}, f32[2048,128]{1,0:T(8,128)}, f32[2,128,128]{2,1,0:T(8,128)}) custom-call(bf16[256,1024]{1,0:T(8,128)(2,1)} %get-tuple-element.9.refs_0_, f32[2048,128]{1,0:T(8,128)} %get-tuple-element.10.refs_1_, f32[2,128,128]{2,1,0:T(8,128)} %get-tuple-element.11.refs_2_), custom_call_target="tpu_custom_call" | custom-call | tf_op jit(solution)/shard_map/results/pallas_call | solution.py:658

commit v4 on v3

--- a/solution.py
+++ b/solution.py
@@ -50,7 +50,7 @@
     queries_hbm, keys_hbm, values_hbm, out_grad_hbm, maps_hbm, first_hbm, second_hbm, gain,
     attention_hbm, new_maps, new_moments,
     queries, keys, values, out_grad, maps, first_old, second_old,
-    gain_row, attention, turned_q, turned_k, turned_fq,
+    gain_row, attention,
     feat_q, feat_k, slope_q, slope_k, raw_part, grad_raw, local_fk,
     states, core_in, chip, row_in, chain_in, chain_out, share_out, summed,
     grads, grads_core, grads_chip, grads_row, grads_part, rows_in,
@@ -117,11 +117,10 @@
     for other in levels:
         greet(index(other, row, core))
 
-    def masked(scores, turned=False):
+    def masked(scores):
         line = lax.broadcasted_iota(jnp.int32, (SPAN, SPAN), 0)
         column = lax.broadcasted_iota(jnp.int32, (SPAN, SPAN), 1)
-        kept = (line <= column) if turned else (line >= column)
-        return jnp.where(kept, scores, 0.0).astype(BF16)
+        return jnp.where(line >= column, scores, 0.0).astype(BF16)
 
     def both(body, pair):
         body(2 * pair)
@@ -413,14 +412,11 @@
     def query_features(head):
         cols = head_rows(head)
         feature(queries, maps[head_rows(head), :], feat_q, slope_q, cols)
-        turned_fq[head_rows(head), :] = feat_q[:, cols].T
 
     def inside(head):
         cols = head_rows(head)
         scores = masked(dot(feat_q[:, cols], feat_k[:, cols], 1, 1))
         raw_part[:, cols] = dot(scores, values[:, cols], 1, 0)
-        turned_q[head_rows(head), :] = queries[:, cols].T
-        turned_k[head_rows(head), :] = keys[:, cols].T
 
     def forward(head):
         cols = head_rows(head)
@@ -434,7 +430,7 @@
         inner = jnp.mean(dunit * unit, -1, keepdims=True)
         grad = (scale * (dunit - unit * inner)).astype(BF16)
         grad_raw[:, cols] = grad
-        states[1, head_rows(head), :] = dot(turned_fq[head_rows(head), :], grad, 1, 0)
+        states[1, head_rows(head), :] = dot(feat_q[:, cols], grad, 0, 0)
 
     def query_side(head):
         cols = head_rows(head)
@@ -442,17 +438,16 @@
         pscores = masked(dot(grad, values[:, cols], 1, 1))
         before = summed[0, head_rows(head), :].astype(BF16)
         grad_fq = dot(grad, before, 1, 1) + dot(pscores, feat_k[:, cols], 1, 0)
-        turned = masked(dot(values[:, cols], grad, 1, 1), True)
-        local_fk[:, cols] = dot(turned, feat_q[:, cols], 1, 0)
+        local_fk[:, cols] = dot(pscores, feat_q[:, cols], 0, 0)
         grad_pq = (grad_fq * slope_q[:, cols]).astype(BF16)
-        grads[0, head_rows(head), :] = dot(turned_q[head_rows(head), :], grad_pq, 1, 0)
+        grads[0, head_rows(head), :] = dot(queries[:, cols], grad_pq, 0, 0)
 
     def key_side(head):
         cols = head_rows(head)
         after = summed[1, head_rows(head), :].astype(BF16)
         grad_fk = dot(values[:, cols], after, 1, 1) + local_fk[:, cols]
         grad_pk = (grad_fk * slope_k[:, cols]).astype(BF16)
-        grads[1, head_rows(head), :] = dot(turned_k[head_rows(head), :], grad_pk, 1, 0)
+        grads[1, head_rows(head), :] = dot(keys[:, cols], grad_pk, 0, 0)
 
     def keys_pair(pair):
         both(key_features, pair)
@@ -558,12 +553,25 @@
     leave.wait()
 
 
-def hand_over(*refs):
-    copies = [pltpu.make_async_copy(refs[i], refs[3 + i], refs[6].at[i]) for i in range(3)]
-    for one in copies:
-        one.start()
-    for one in copies:
-        one.wait()
+def hand_over(sources, targets, staged, arrive, leave):
+    moves = []
+    for source, target, stage in zip(sources, targets, staged):
+        rows = source.shape[0]
+        size = min(rows, max(rows // 4, SPAN // 2))
+        for start in range(0, rows, size):
+            here = pl.ds(start, size)
+            slot = len(moves)
+            moves.append((
+                pltpu.make_async_copy(source.at[here], stage.at[here], arrive.at[slot]),
+                pltpu.make_async_copy(stage.at[here], target.at[here], leave.at[slot]),
+            ))
+    for into, _ in moves:
+        into.start()
+    for into, out in moves:
+        into.wait()
+        out.start()
+    for _, out in moves:
+        out.wait()
 
 
 def local(count, queries, keys, values, out_grad, maps, gain, first_moment, second_moment):
@@ -576,7 +584,6 @@
     square = (2, PAIRS, E, E)
     dma = pltpu.SemaphoreType.DMA
     chunks = half * width
-    turned = (H * E, SPAN)
     scratch = [
         pltpu.VMEM(wide, BF16),
         pltpu.VMEM(wide, BF16),
@@ -587,9 +594,6 @@
         pltpu.VMEM((share, E), F32),
         pltpu.VMEM((1, H * E), F32),
         pltpu.VMEM(wide, BF16),
-        pltpu.VMEM(turned, BF16),
-        pltpu.VMEM(turned, BF16),
-        pltpu.VMEM(turned, BF16),
         pltpu.VMEM(wide, BF16),
         pltpu.VMEM(wide, BF16),
         pltpu.VMEM(wide, F32),
@@ -656,11 +660,12 @@
     )
     results = (attention, new_maps, new_moments)
     attention, new_maps, new_moments = pl.pallas_call(
-        hand_over,
+        lambda *refs: hand_over(refs[:3], refs[3:6], refs[6:9], *refs[9:]),
         out_shape=tuple(jax.ShapeDtypeStruct(one.shape, one.dtype) for one in results),
         in_specs=[anywhere] * 3,
         out_specs=(anywhere,) * 3,
-        scratch_shapes=[dma((3,))],
+        scratch_shapes=[pltpu.VMEM(one.shape, one.dtype) for one in results]
+        + [dma((8,)), dma((8,))],
         compiler_params=pltpu.CompilerParams(vmem_limit_bytes=63 * 1024 * 1024),
         name="results",
     )(*results)

time: 128 us -> 77.5 us (0.61)
  Pallas kernels: 126 us -> 75.9 us
    pallas_call x1, Pallas kernels: 52.7 us -> 2.26 us  [local(): pl.pallas_call(lambda *refs: hand_over(refs[:3], refs[3:6], refs[6:9], *r...]
where the time goes in v4:
time: 77.5 us; the launch traced here: 76.5 us
  Pallas kernels  75.9 us (98%)
    pallas_call x1, Pallas kernels, local(): pl.pallas_call(functools.partial(kernel, depth, width, share), out_shape=...  73.6 us
    pallas_call x1, Pallas kernels, local(): pl.pallas_call(lambda *refs: hand_over(refs[:3], refs[3:6], refs[6:9], *r...  2.26 us

profile of v4, /device:TPU:0, one launch (start us, length us, event | category | flops | bytes accessed | tf_op | source)
XLA Modules:
  0.0 76.5 jit_solution(9346182420449702993)
XLA Ops:
  0.6 73.6 %layer.1 = (bf16[256,1024]{1,0:T(8,128)(2,1)}, f32[2048,128]{1,0:T(8,128)}, f32[2,128,128]{2,1,0:T(8,128)}) custom-call(bf16[256,1024]{1,0:T(8,128)(2,1)} %queries_hbm.1, bf16[256,1024]{1,0:T(8,128)(2,1)} %keys_hbm.1, bf16[256,1024]{1,0:T(8,128)(2,1)} %values_hbm.1, bf16[256,1024]{1,0:T(8,128)(2,1)} %out_grad_hbm.1, f32[2048,128]{1,0:T(8,128)} %bitcast.2, ...), custom_call_target="tpu_custom_call" | custom-call | tf_op jit(solution)/shard_map/layer/pallas_call | solution.py:643
  74.2 2.3 %results.1 = (bf16[256,1024]{1,0:T(8,128)(2,1)}, f32[2048,128]{1,0:T(8,128)}, f32[2,128,128]{2,1,0:T(8,128)}) custom-call(bf16[256,1024]{1,0:T(8,128)(2,1)} %get-tuple-element.9.refs_0_, f32[2048,128]{1,0:T(8,128)} %get-tuple-element.10.refs_1_, f32[2,128,128]{2,1,0:T(8,128)} %get-tuple-element.11.refs_2_), custom_call_target="tpu_custom_call" | custom-call | tf_op jit(solution)/shard_map/results/pallas_call | solution.py:662

commit v5 on v4

--- a/solution.py
+++ b/solution.py
@@ -348,8 +348,15 @@
                 gradient, maps[mine, :], first_old[...], second_old[...]
             )
             new_maps[mine, :] = rows_new
+            if side == 0:
+                for which in range(half):
+                    owner_copy(1, which).wait_send()
             for other in levels:
                 map_level_copy(side, other).start()
+            own = level - side * half
+            for beside in rows_beside:
+                map_row_copy(side, own, beside).start()
+            map_core_copy(side, own, row).start()
             new_moments[0] = first_new
             new_moments[1] = second_new
 
@@ -359,10 +366,9 @@
             @pl.when(level != side * half + which)
             def _():
                 map_level_arrival(side, which).wait_recv()
-
-            for beside in rows_beside:
-                map_row_copy(side, which, beside).start()
-            map_core_copy(side, which, row).start()
+                for beside in rows_beside:
+                    map_row_copy(side, which, beside).start()
+                map_core_copy(side, which, row).start()
 
     def spread_core(side):
         for which in range(half):
@@ -389,7 +395,11 @@
             for of_row in range(width):
                 map_core_copy(side, which, of_row).wait_send()
 
-            @pl.when(level != side * half + which)
+            passed = level != side * half + which
+            if side == 1:
+                passed = jnp.logical_and(passed, level >= half)
+
+            @pl.when(passed)
             def _():
                 owner_copy(side, which).wait_send()
 
@@ -463,6 +473,10 @@
     def query_pair(pair):
         both(query_side, pair)
         reduce_start(0, pair)
+
+    def reduce_queries():
+        for which in range(half):
+            reduce_levels(0, which)
 
     def key_pair(pair):
         share_arrival(1, pair).wait_recv()
@@ -503,35 +517,30 @@
     scan_rows(1, 0)
     forward_pair(2)
     scan_rows(1, 1)
-    scan_levels(1, 0, True)
     forward_pair(3)
     leave = pltpu.make_async_copy(attention, attention_hbm, store)
     leave.start()
     scan_rows(1, 2)
-    scan_levels(1, 1, True)
+    scan_levels(1, 0, True)
     query_pair(0)
     scan_rows(1, 3)
+    scan_levels(1, 1, True)
+    query_pair(1)
     scan_levels(1, 2, True)
-    query_pair(1)
+    query_pair(2)
     scan_levels(1, 3, True)
-    reduce_rows(0, 0)
-    query_pair(2)
-    reduce_rows(0, 1)
     query_pair(3)
+    for pair in range(PAIRS):
+        reduce_rows(0, pair)
+    pl.when(level < half)(reduce_queries)
     scan_levels(1, 0, False)
-    reduce_rows(0, 2)
-    reduce_rows(0, 3)
     scan_levels(1, 1, False)
-    for which in range(half // 2):
-        reduce_levels(0, which)
     scan_levels(1, 2, False)
-    for which in range(half // 2, half):
-        reduce_levels(0, which)
     key_pair(0)
     scan_levels(1, 3, False)
+    pl.when(level >= half)(reduce_queries)
     key_pair(1)
     reduce_rows(1, 0)
-    update(0)
     key_pair(2)
     reduce_rows(1, 1)
     key_pair(3)
@@ -539,8 +548,9 @@
     reduce_rows(1, 3)
     for which in range(half):
         reduce_levels(1, which)
+    update(0)
+    update(1)
     spread(0)
-    update(1)
     spread_core(0)
     spread(1)
     spread_core(1)

time: 77.5 us -> 73.6 us (0.950)
  Pallas kernels: 75.9 us -> 71.7 us
    pallas_call x1, Pallas kernels: 73.6 us -> 69.5 us  [local(): pl.pallas_call(functools.partial(kernel, depth, width, share), out_shape=...]
where the time goes in v5:
time: 73.6 us; the launch traced here: 72.4 us
  Pallas kernels  71.7 us (97%)
    pallas_call x1, Pallas kernels, local(): pl.pallas_call(functools.partial(kernel, depth, width, share), out_shape=...  69.5 us
    pallas_call x1, Pallas kernels, local(): pl.pallas_call(lambda *refs: hand_over(refs[:3], refs[3:6], refs[6:9], *r...  2.26 us

profile of v5, /device:TPU:0, one launch (start us, length us, event | category | flops | bytes accessed | tf_op | source)
XLA Modules:
  0.0 72.4 jit_solution(5032621653403609673)
XLA Ops:
  0.6 69.5 %layer.1 = (bf16[256,1024]{1,0:T(8,128)(2,1)}, f32[2048,128]{1,0:T(8,128)}, f32[2,128,128]{2,1,0:T(8,128)}) custom-call(bf16[256,1024]{1,0:T(8,128)(2,1)} %queries_hbm.1, bf16[256,1024]{1,0:T(8,128)(2,1)} %keys_hbm.1, bf16[256,1024]{1,0:T(8,128)(2,1)} %values_hbm.1, bf16[256,1024]{1,0:T(8,128)(2,1)} %out_grad_hbm.1, f32[2048,128]{1,0:T(8,128)} %bitcast.2, ...), custom_call_target="tpu_custom_call" | custom-call | tf_op jit(solution)/shard_map/layer/pallas_call | solution.py:653
  70.1 2.3 %results.1 = (bf16[256,1024]{1,0:T(8,128)(2,1)}, f32[2048,128]{1,0:T(8,128)}, f32[2,128,128]{2,1,0:T(8,128)}) custom-call(bf16[256,1024]{1,0:T(8,128)(2,1)} %get-tuple-element.9.refs_0_, f32[2048,128]{1,0:T(8,128)} %get-tuple-element.10.refs_1_, f32[2,128,128]{2,1,0:T(8,128)} %get-tuple-element.11.refs_2_), custom_call_target="tpu_custom_call" | custom-call | tf_op jit(solution)/shard_map/results/pallas_call | solution.py:672

commit v6 on v5

--- a/solution.py
+++ b/solution.py
@@ -376,6 +376,10 @@
                 map_row_arrival(side, which, beside).wait_recv()
                 map_core_copy(side, which, beside).start()
 
+    def spread_queries():
+        spread(0)
+        spread_core(0)
+
     def spread_end(side):
         for which in range(half):
             for of_row in range(width):
@@ -410,7 +414,7 @@
 
     def feature(source, weights, feat, slope, cols):
         pre = dot(source[:, cols], weights.astype(BF16), 1, 0)
-        sigmoid = 1.0 / (1.0 + jnp.exp(-pre))
+        sigmoid = 0.5 + 0.5 * jnp.tanh(0.5 * pre)
         feat[:, cols] = (pre * sigmoid).astype(BF16)
         slope[:, cols] = sigmoid * (1.0 + pre * (1.0 - sigmoid))
 
@@ -550,10 +554,10 @@
         reduce_levels(1, which)
     update(0)
     update(1)
-    spread(0)
-    spread_core(0)
+    pl.when(level < half)(spread_queries)
     spread(1)
     spread_core(1)
+    pl.when(level >= half)(spread_queries)
     spread_end(0)
     spread_end(1)
     scan_drain(0)

time: 73.6 us -> 75.5 us (1.026)
  the two profiles are of different devices: /device:TPU:0 before, /device:TPU:17 now
where the time goes in v6:
time: 75.5 us; the launch traced here: 75.3 us
  Pallas kernels  74.6 us (99%)
    pallas_call x1, Pallas kernels, local(): pl.pallas_call(functools.partial(kernel, depth, width, share), out_shape=...  72.4 us
    pallas_call x1, Pallas kernels, local(): pl.pallas_call(lambda *refs: hand_over(refs[:3], refs[3:6], refs[6:9], *r...  2.26 us

profile of v6, /device:TPU:17, one launch (start us, length us, event | category | flops | bytes accessed | tf_op | source)
XLA Modules:
  0.0 75.3 jit_solution(2602953740428237401)
XLA Ops:
  0.6 72.4 %layer.1 = (bf16[256,1024]{1,0:T(8,128)(2,1)}, f32[2048,128]{1,0:T(8,128)}, f32[2,128,128]{2,1,0:T(8,128)}) custom-call(bf16[256,1024]{1,0:T(8,128)(2,1)} %queries_hbm.1, bf16[256,1024]{1,0:T(8,128)(2,1)} %keys_hbm.1, bf16[256,1024]{1,0:T(8,128)(2,1)} %values_hbm.1, bf16[256,1024]{1,0:T(8,128)(2,1)} %out_grad_hbm.1, f32[2048,128]{1,0:T(8,128)} %bitcast.2, ...), custom_call_target="tpu_custom_call" | custom-call | tf_op jit(solution)/shard_map/layer/pallas_call | solution.py:657
  73.0 2.3 %results.1 = (bf16[256,1024]{1,0:T(8,128)(2,1)}, f32[2048,128]{1,0:T(8,128)}, f32[2,128,128]{2,1,0:T(8,128)}) custom-call(bf16[256,1024]{1,0:T(8,128)(2,1)} %get-tuple-element.9.refs_0_, f32[2048,128]{1,0:T(8,128)} %get-tuple-element.10.refs_1_, f32[2,128,128]{2,1,0:T(8,128)} %get-tuple-element.11.refs_2_), custom_call_target="tpu_custom_call" | custom-call | tf_op jit(solution)/shard_map/results/pallas_call | solution.py:676
